TPU v7x, 128 devices: a whole 4x4x4 slice. The times are simulated.
128 devices in a mesh: row: 16 (over y, x), col: 8 (over z, core).
Axes of the slice: x: 4, y: 4, z: 4, core: 2. Of those that a mesh axis runs over, the one named last changes fastest.
Arguments:
- embeddings: bfloat16 [24576, 1024], P(None, ('row', 'col')), may hold values from -6 to 6
- inv_scale: float32 [1024], replicated, may hold values from 0.5 to 2
- noise: float32 [24576], replicated, may hold values from 0.5 to 2
Outputs:
- factor: float32 [12, 16, 128, 1024], P(None, 'row', None, 'col')
- schur: float32 [12, 16, 128, 24, 8, 128], P(None, 'row', None, None, 'col')
All inputs are finite; a program needn't handle non-finite values.
Results may differ from a plain program's by a relative error of at most 0.0027.
Values may be sent and summed in bfloat16 or wider, within the bound.
A program may use at most 192 MiB of HBM per device.

v0:
```python
import jax
import jax.numpy as jnp
from jax import lax
from jax.sharding import PartitionSpec as P

TILE = 128
PB = 512
PANELS = 2


def from_root(shard, axis, root):
    mine = lax.axis_index(axis) == root
    return lax.psum(jnp.where(mine, shard, jnp.zeros_like(shard)), axis)


def trailing_update(left_rows, right_rows):
    return lax.dot_general(
        left_rows,
        right_rows,
        (((1,), (1,)), ((), ())),
        precision=lax.Precision.HIGHEST,
        preferred_element_type=jnp.float32,
    )


def body(embeddings, inv_scale, noise):
    nrow = lax.axis_size("row")
    ncol = lax.axis_size("col")
    prow = lax.axis_index("row")
    qcol = lax.axis_index("col")
    total, fdev = embeddings.shape
    width = inv_scale.shape[0]
    crow = total // (TILE * nrow)
    ccol = total // (TILE * ncol)
    sub_row = TILE // ncol
    sub_col = TILE // nrow
    per_panel = PB // TILE
    lead = PANELS * PB
    scale_part = lax.dynamic_slice_in_dim(inv_scale, (prow * ncol + qcol) * fdev, fdev)
    scaled = (embeddings.astype(jnp.float32) * scale_part[None, :]).astype(jnp.bfloat16)
    row_part = (
        scaled.reshape(crow, nrow, ncol, sub_row, fdev)
        .transpose(1, 2, 0, 3, 4)
        .reshape(nrow * ncol, crow, sub_row, fdev)
    )
    col_part = (
        scaled.reshape(ccol, ncol, nrow, sub_col, fdev)
        .transpose(2, 1, 0, 3, 4)
        .reshape(nrow * ncol, ccol, sub_col, fdev)
    )
    row_mine, col_mine = (
        lax.all_to_all(row_part, ("row", "col"), split_axis=0, concat_axis=3, tiled=True),
        lax.all_to_all(col_part, ("row", "col"), split_axis=0, concat_axis=3, tiled=True),
    )
    row_vecs = lax.all_gather(row_mine[0], "col", axis=1, tiled=True).reshape(crow * TILE, width)
    row_sq = jnp.sum(jnp.square(row_vecs.astype(jnp.float32)), axis=1)
    rows_global = (
        (jnp.arange(crow, dtype=jnp.int32)[:, None] * nrow + prow) * TILE
        + jnp.arange(TILE, dtype=jnp.int32)[None, :]
    ).reshape(-1)
    row_noise = jnp.take(noise, rows_global)
    cols_global = (
        (jnp.arange(ccol, dtype=jnp.int32)[:, None] * ncol + qcol) * TILE
        + jnp.arange(TILE, dtype=jnp.int32)[None, :]
    ).reshape(-1)
    piece = lax.all_gather(col_mine[0], "row", axis=1, tiled=True)
    count = piece.shape[1]
    flat = piece.reshape(ccol * count, width)
    col_sq = jnp.sum(jnp.square(flat.astype(jnp.float32)), axis=1)
    inner = lax.dot_general(
        row_vecs, flat, (((1,), (1,)), ((), ())), preferred_element_type=jnp.float32
    )
    dist = row_sq[:, None] + col_sq[None, :] - 2.0 * inner
    kern = jnp.exp(dist * (-0.5 / width))
    piece_cols = (
        (jnp.arange(ccol, dtype=jnp.int32)[:, None] * ncol + qcol) * TILE
        + jnp.arange(count, dtype=jnp.int32)[None, :]
    ).reshape(-1)
    same = rows_global[:, None] == piece_cols[None, :]
    kern = kern + jnp.where(same, row_noise[:, None], jnp.zeros_like(kern))
    matrix = kern.reshape(crow * TILE, ccol, count).reshape(crow * TILE, ccol * TILE)

    def share_panel(columns, first_block, k):
        blocks = columns.shape[1] // TILE
        view = columns.reshape(crow * TILE, blocks, TILE)
        pieces = []
        for unit in range(k * per_panel, (k + 1) * per_panel):
            owned = view[:, unit // ncol - first_block, :]
            pieces.append(jnp.where(qcol == unit % ncol, owned, jnp.zeros_like(owned)))
        term = jnp.concatenate(pieces, axis=1)
        panel = lax.psum(term, "col")
        return jnp.where((rows_global < k * PB)[:, None], jnp.zeros_like(panel), panel)

    factors = []
    panel = share_panel(matrix, 0, 0)
    for k in range(PANELS):
        stacked = panel.reshape(crow, TILE, PB)
        factor_pieces = []
        for factor_unit in range(k * per_panel, (k + 1) * per_panel):
            factor_owned = stacked[factor_unit // nrow]
            factor_pieces.append(
                jnp.where(prow == factor_unit % nrow, factor_owned, jnp.zeros_like(factor_owned))
            )
        diagonal = lax.psum(jnp.concatenate(factor_pieces, axis=0), "row")
        chol = jnp.linalg.cholesky(diagonal)
        left_rows = jax.scipy.linalg.solve_triangular(chol, panel.T, lower=True).T
        received = []
        for turn in range(nrow // ncol):
            root = qcol + turn * ncol
            got = from_root(left_rows, "row", root)
            received.append(got.reshape(crow, TILE, PB))
        right_rows = jnp.stack(received, axis=1).reshape(ccol * TILE, PB)
        left_rows, right_rows = (left_rows, right_rows)
        factors.append(left_rows)
        matrix = matrix - trailing_update(left_rows, right_rows)
        if k + 1 < PANELS:
            panel = share_panel(matrix, 0, k + 1)
    factor_all = jnp.concatenate(factors, axis=1)
    share_width = lead // ncol
    factor_mine = lax.dynamic_slice_in_dim(factor_all, qcol * share_width, share_width, 1)
    dead = (rows_global[:, None] < lead) | (cols_global[None, :] < lead)
    schur = jnp.where(dead, jnp.zeros_like(matrix), matrix)
    return (
        factor_mine.reshape(crow, 1, TILE, share_width),
        schur.reshape(crow, 1, TILE, ccol, 1, TILE),
    )


def solution(mesh):
    placed = (P(None, ("row", "col")), P(), P())
    return jax.shard_map(
        body,
        mesh=mesh,
        in_specs=placed,
        out_specs=(P(None, "row", None, "col"), P(None, "row", None, None, "col", None)),
        check_vma=False,
    )
```

profile of v0, /device:TPU:1, one launch (start us, length us, event | category | flops | bytes accessed | tf_op | source)
XLA Modules:
  0.0 1283.1 jit_solution(398813368300098269)
XLA Ops:
  21.2 23.8 %all_to_all.30 = bf16[128,2,768]{2,1,0:T(2,128)(2,1)} all-to-all(bf16[128,2,768]{2,1,0:T(2,128)(2,1)} %reshape.277), channel_id=1, replica_groups=mesh['row'=16,'col'=8] {'row','col'}, dimensions={0} | all-to-all | bytes 786432 | tf_op jit(solution)/shard_map/all_to_all | solution.py:52
  55.3 10.4 reshape.237
  76.2 16.6 %all_to_all.31 = bf16[128,2,768]{2,1,0:T(2,128)(2,1)S(1)} all-to-all(bf16[128,2,768]{2,1,0:T(2,128)(2,1)S(1)} %reshape.279), channel_id=1, replica_groups=mesh['row'=16,'col'=8] {'row','col'}, dimensions={0} | all-to-all | bytes 786432 | tf_op jit(solution)/shard_map/all_to_all | solution.py:53
  111.5 46.1 %all-gather.5.cloned.1.call-done = bf16[24,128,1024]{2,0,1:T(8,128)(2,1)} async-done(((bf16[24,8,1024]{2,0,1:T(8,128)(2,1)}), bf16[24,128,1024]{2,0,1:T(8,128)(2,1)}) %all-gather.5.cloned.1.call-update) | async-done | bytes 6291472 | tf_op jit(solution)/shard_map/all_gather | solution.py:66
  168.3 16.2 %select_add_fusion = f32[1536,3072]{1,0:T(8,128)} fusion(bf16[1536,1024]{1,0:T(8,128)(2,1)S(1)} %bitcast.230, bf16[3072,1024]{1,0:T(8,128)(2,1)S(1)} %bitcast.229, f32[1536]{0:T(1024)S(1)} %fusion.67, s32[3072]{0:T(1024)S(1)} %add_bitcast_fusion, f32[3072]{0:T(1024)S(1)} %bitcast.232, f32[1536]{0:T(1024)S(1)} %bitcast.233, s32[1536]{0:T(1024)S(1)} %get-tuple-element.97), kind=kOutput, calls=%fused_computation.6 | convolution fusion | flops 9696706560 | bytes 28354560 | tf_op jit(solution)/shard_map/dot_general | solution.py:70
  184.5 18.7 %copy.74 = f32[1536,3072]{0,1:T(8,128)} copy(f32[1536,3072]{1,0:T(8,128)} %select_add_fusion) | data formatting | bytes 37748736 | tf_op jit(solution)/shard_map/add | solution.py:80
  206.7 67.2 %all-reduce.10.cloned.1.call-done = f32[1536,512]{0,1:T(8,128)} async-done(((f32[1536,512]{0,1:T(8,128)}), f32[1536,512]{0,1:T(8,128)}) %all-reduce.10.cloned.1.call-update) | async-done | bytes 3145744 | tf_op jit(solution)/shard_map/psum | solution.py:91
  280.3 84.0 %all-reduce.12.cloned.1.call-done = f32[512,512]{0,1:T(8,128)} async-done(((f32[512,512]{0,1:T(8,128)}), f32[512,512]{0,1:T(8,128)}) %all-reduce.12.cloned.1.call-update) | async-done | bytes 1048592 | tf_op jit(solution)/shard_map/psum | solution.py:104
  367.3 11.7 cholesky.286
  379.1 9.8 custom-call.27
  389.7 11.7 cholesky.305
  401.4 10.0 custom-call.28
  412.1 11.7 cholesky.326
  424.4 9.8 custom-call.29
  434.8 12.1 cholesky.343
  458.5 39.3 %custom-call.30 = f32[4,128,128]{1,2,0:T(8,128)S(1)} custom-call(f32[4,128,128]{2,1,0:T(8,128)S(1)} %get-tuple-element.18), custom_call_target="InvertDiagBlocksLowerTriangular" | custom-call | tf_op jit(solution)/shard_map/jit(_solve_triangular)/triangular_solve | solution.py:106
  522.0 123.1 %all-reduce.20.cloned.1.call-done = (f32[12,1,128,512]{3,2,0,1:T(8,128)}, f32[12,1,128,512]{3,2,0,1:T(8,128)}) async-done(((f32[12,1,128,512]{3,2,0,1:T(8,128)}, f32[12,1,128,512]{3,2,0,1:T(8,128)}), (f32[12,1,128,512]{3,2,0,1:T(8,128)}, f32[12,1,128,512]{3,2,0,1:T(8,128)})) %all-reduce.20.cloned.1.call-update) | async-done | bytes 6291472 | tf_op jit(solution)/shard_map/psum | solution.py:13
  649.7 64.5 %convolution_subtract_fusion = f32[1536,3072]{1,0:T(8,128)} fusion(f32[1536,3072]{1,0:T(8,128)} %select_add_fusion, f32[3072,512]{1,0:T(8,128)S(1)} %bitcast.219, f32[128,1536]{1,0:T(8,128)S(1)} %fusion.47, f32[128,1536]{1,0:T(8,128)S(1)} %fusion.48, f32[128,1536]{1,0:T(8,128)S(1)} %fusion.50, f32[128,1536]{1,0:T(8,128)S(1)} %fusion.23), kind=kOutput, calls=%fused_computation.8 | convolution fusion | flops 28998107136 | bytes 47185920 | tf_op jit(solution)/shard_map/dot_general | solution.py:17
  714.2 18.7 %copy.79 = f32[1536,3072]{0,1:T(8,128)} copy(f32[1536,3072]{1,0:T(8,128)} %convolution_subtract_fusion) | data formatting | bytes 37748736 | tf_op jit(solution)/shard_map/sub | solution.py:115
  736.3 67.4 %all-reduce.14.cloned.1.call-done = f32[1536,512]{0,1:T(8,128)} async-done(((f32[1536,512]{0,1:T(8,128)}), f32[1536,512]{0,1:T(8,128)}) %all-reduce.14.cloned.1.call-update) | async-done | bytes 3145744 | tf_op jit(solution)/shard_map/psum | solution.py:91
  810.9 83.3 %all-reduce.16.cloned.1.call-done = f32[512,512]{0,1:T(8,128)} async-done(((f32[512,512]{0,1:T(8,128)}), f32[512,512]{0,1:T(8,128)}) %all-reduce.16.cloned.1.call-update) | async-done | bytes 1048592 | tf_op jit(solution)/shard_map/psum | solution.py:104
  898.2 11.7 cholesky.358
  910.6 9.8 custom-call.31
  923.1 11.7 cholesky.377
  935.5 10.0 custom-call.32
  947.0 11.7 cholesky.398
  970.8 12.0 cholesky.415
  987.0 11.4 while.5
  998.4 39.3 %custom-call.34 = f32[4,128,128]{1,2,0:T(8,128)S(1)} custom-call(f32[4,128,128]{2,1,0:T(8,128)S(1)} %get-tuple-element.19), custom_call_target="InvertDiagBlocksLowerTriangular" | custom-call | tf_op jit(solution)/shard_map/jit(_solve_triangular)/triangular_solve | solution.py:106
  1063.2 119.7 %all-reduce.18.cloned.1.call-done = (f32[12,1,128,512]{3,2,0,1:T(8,128)}, f32[12,1,128,512]{3,2,0,1:T(8,128)}) async-done(((f32[12,1,128,512]{3,2,0,1:T(8,128)}, f32[12,1,128,512]{3,2,0,1:T(8,128)}), (f32[12,1,128,512]{3,2,0,1:T(8,128)}, f32[12,1,128,512]{3,2,0,1:T(8,128)})) %all-reduce.18.cloned.1.call-update) | async-done | bytes 6291472 | tf_op jit(solution)/shard_map/psum | solution.py:13
  1187.9 70.3 %select_bitcast_fusion = f32[192,8,24,128]{3,1,2,0:T(8,128)} fusion(f32[1536,3072]{1,0:T(8,128)} %convolution_subtract_fusion, f32[3072,512]{1,0:T(8,128)S(1)} %bitcast.217, pred[3072]{0:T(1024)(128)(4,1)S(1)} %broadcast_compare_fusion, pred[1536]{0:T(1024)(128)(4,1)S(1)} %get-tuple-element.94, f32[128,1536]{1,0:T(8,128)S(1)} %copy-done.11, ...), kind=kOutput, calls=%fused_computation.5 | convolution fusion | flops 29007544320 | bytes 47190528 | tf_op jit(solution)/shard_map/dot_general | solution.py:17
  1258.2 17.9 %copy.89 = f32[192,8,24,128]{3,2,1,0:T(8,128)} copy(f32[192,8,24,128]{3,1,2,0:T(8,128)} %select_bitcast_fusion) | data formatting | bytes 37748736
  (189 shorter events, 200.2 us)
Async XLA Ops:
  7.2 93.2 %copy-start = (f32[24576]{0:T(1024)S(1)}, f32[24576]{0:T(1024)}, u32[]{:S(2)}) copy-start(f32[24576]{0:T(1024)} %param.8) | copy-start | bytes 294916
  7.2 101.8 %all-gather.3.cloned.1.call-start = ((), (), s32[]{:S(2)}) async-start(), calls=%async_computation.2 | async-start | bytes 3538944 | tf_op jit(solution)/shard_map/all_gather | solution.py:55
  9.1 0.7 copy-start.12
  51.2 4.1 copy-start.13
  55.1 102.6 %all-gather.5.cloned.1.call-start = ((), (), s32[]{:S(2)}) async-start(), calls=%async_computation.3 | async-start | bytes 6684672 | tf_op jit(solution)/shard_map/all_gather | solution.py:66
  100.0 174.0 %all-reduce.10.cloned.1.call-start = ((), (), s32[]{:S(2)}) async-start(), calls=%async_computation.4 | async-start | bytes 6291456 | tf_op jit(solution)/shard_map/psum | solution.py:91
  161.8 6.5 copy-start.14
  206.6 157.7 %all-reduce.12.cloned.1.call-start = ((), (), s32[]{:S(2)}) async-start(), calls=%async_computation.5 | async-start | bytes 2097152 | tf_op jit(solution)/shard_map/psum | solution.py:104
  276.1 2.3 copy-start.7
  277.3 367.8 %all-reduce.20.cloned.1.call-start = ((), (), s32[]{:S(2)}) async-start(), calls=%async_computation.9 | async-start | bytes 12582912 | tf_op jit(solution)/shard_map/psum | solution.py:13
  497.8 4.9 copy-start.16
  506.5 143.2 %copy-start.2 = (f32[128,1536]{1,0:T(8,128)}, f32[128,1536]{1,0:T(8,128)S(1)}, u32[]{:S(2)}) copy-start(f32[128,1536]{1,0:T(8,128)S(1)} %fusion.48) | copy-start | bytes 2359300
  511.2 138.5 %copy-start.8 = (f32[128,1536]{1,0:T(8,128)}, f32[128,1536]{1,0:T(8,128)S(1)}, u32[]{:S(2)}) copy-start(f32[128,1536]{1,0:T(8,128)S(1)} %fusion.47) | copy-start | bytes 2359300
  521.9 281.8 %all-reduce.14.cloned.1.call-start = ((), (), s32[]{:S(2)}) async-start(), calls=%async_computation.6 | async-start | bytes 6291456 | tf_op jit(solution)/shard_map/psum | solution.py:91
  736.3 157.9 %all-reduce.16.cloned.1.call-start = ((), (), s32[]{:S(2)}) async-start(), calls=%async_computation.7 | async-start | bytes 2097152 | tf_op jit(solution)/shard_map/psum | solution.py:104
  807.0 375.9 %all-reduce.18.cloned.1.call-start = ((), (), s32[]{:S(2)}) async-start(), calls=%async_computation.8 | async-start | bytes 12582912 | tf_op jit(solution)/shard_map/psum | solution.py:13
  897.2 1.0 copy-start.15
  1037.8 5.0 copy-start.6
  1045.5 7.1 copy-start.3
  1049.1 3.5 copy-start.9
  1059.8 1.7 copy-start.4
  1059.8 1.8 copy-start.10
  1186.5 1.1 copy-start.5
  1186.5 1.4 copy-start.11
  1258.2 17.9 %copy-start.1 = (f32[24576]{0:T(1024)S(1)}, f32[24576]{0:T(1024)}, u32[]{:S(2)}) copy-start(f32[24576]{0:T(1024)} %param.8) | copy-start | bytes 294916
Sparse Core Ops, SparseCore 0:
  55.2 24.6 all-gather.2
  100.1 57.5 all-gather.4
  206.7 67.1 all-reduce.9
  277.4 86.8 all-reduce.11
  522.1 123.0 all-reduce.19
  736.4 67.2 all-reduce.13
  807.3 86.8 all-reduce.15
  1059.8 122.9 all-reduce.17
where the time goes:
time: 1290 us; the launch traced here: 1280 us
  waiting for transfers between devices  591 us (46%)
  other arithmetic  285 us (22%)
  matrix products  183 us (14%)
  local copies, waits for them, and re-layouts  163 us (13%)
  blocking collectives  40.4 us (3%)
  between operations  20 us (2%)
    psum x2, waiting for transfers between devices, from_root(): return lax.psum(jnp.where(mine, shard, jnp.zeros_like(shard)), axis)  243 us
    psum x2, waiting for transfers between devices, body(): diagonal = lax.psum(jnp.concatenate(factor_pieces, axis=0), 'row')  167 us
    another operation x29, other arithmetic, body(): chol = jnp.linalg.cholesky(diagonal)  158 us
    dot_general x2, matrix products, trailing_update(): lax.dot_general(left_rows, right_rows, (((1,), (1,)), ((), ())), precisio...  135 us
    psum x2, waiting for transfers between devices, share_panel(): panel = lax.psum(term, 'col')  135 us
    another operation x5, other arithmetic, body(): left_rows = jax.scipy.linalg.solve_triangular(chol, panel.T, lower=True).T  79.9 us
    all_gather x1, waiting for transfers between devices, body(): piece = lax.all_gather(col_mine[0], 'row', axis=1, tiled=True)  46.1 us
    unnamed x39, local copies, waits for them, and re-layouts  33.4 us
  transfers between devices with their start and end apart: 8, of which 7 were waited for; matrix products, arithmetic and copies ran while one was open for 4% of the time, Pallas kernels for 0%

commit v1 on v0

v1 whole, which is shorter than its diff:
```python
import functools
import math

import jax
import jax.numpy as jnp
from jax import lax
from jax.experimental import pallas as pl
from jax.experimental.pallas import tpu as pltpu
from jax.sharding import PartitionSpec as P

TILE = 128
PB = 512
PANELS = 2
B=128
def factor_block(load, store):
    lane = lax.broadcasted_iota(jnp.int32, (8, B), 1)
    sub = lax.broadcasted_iota(jnp.int32, (8, B), 0)
    X = [load(g) for g in range(B // 8)]
    for g in range(B // 8):
        P = X[g]
        base = 8 * g
        c = [jnp.broadcast_to(P[:, base + j:base + j + 1], (8, B)) for j in range(8)]
        s = [[jnp.broadcast_to(c[j][i:i + 1, :], (8, B)) if j <= i else None for j in range(8)] for i in range(8)]
        ingroup = (lane >= base) & (lane < base + 8)
        Pp = jnp.where(ingroup, jnp.where(lane - base == sub, 1.0, 0.0), P)
        r = [jnp.broadcast_to(Pp[k:k + 1, :], (8, B)) for k in range(8)]
        l = [[None] * 8 for _ in range(8)]
        dinv = [None] * 8
        for k in range(8):
            dinv[k] = 1.0 / s[k][k]
            for i in range(k + 1, 8):
                l[i][k] = s[i][k] * dinv[k]
                for j in range(k + 1, i + 1):
                    s[i][j] = s[i][j] - l[i][k] * s[j][k]
        f = []
        for k in range(8):
            v = r[k]
            for m in range(k):
                v = v - l[k][m] * f[m]
            f.append(v)
        w = [None] * 8
        for k in range(7, -1, -1):
            v = f[k] * dinv[k]
            for m in range(k + 1, 8):
                v = v - l[m][k] * w[m]
            w[k] = v
        fo, so = f[0], s[0][0]
        for k in range(1, 8):
            fo = jnp.where(sub == k, f[k], fo)
            so = jnp.where(sub == k, s[k][k], so)
        store(g, fo * lax.rsqrt(so))
        for i in range(g + 1, B // 8):
            Xi = X[i]
            acc = jnp.where(ingroup, 0.0, Xi)
            for k in range(8):
                acc = acc - jnp.broadcast_to(Xi[:, base + k:base + k + 1], (8, B)) * w[k]
            X[i] = acc

def split(x):
    hi = x.astype(jnp.bfloat16)
    return hi, (x - hi.astype(jnp.float32)).astype(jnp.bfloat16)

def dot(a, b):
    return jnp.dot(a, b, preferred_element_type=jnp.float32)

def dot3(a, b):
    ah, al = a; bh, bl = b
    return dot(ah, bh) + dot(ah, bl) + dot(al, bh)

LOG2E = math.log2(math.e)

def chol_body(zl_ref, noise_ref, w_ref, wt_ref, X, V, zt, n, width):
    nb = n // B
    zt[...] = zl_ref[...].T
    zf = zl_ref[...].astype(jnp.float32)
    hc = jnp.sum(zf * zf, axis=0, keepdims=True) * (LOG2E / (2 * width))
    hcol = jnp.broadcast_to(hc, (8, n)).T[:, 0:1]
    for i in range(nb):
        rows = slice(i * B, (i + 1) * B)
        t = dot(zt[rows, :], zl_ref[...]) * (LOG2E / width) - hcol[rows, :] - hc
        k = jnp.exp2(t)
        ri = lax.broadcasted_iota(jnp.int32, (B, n), 0) + i * B
        ci = lax.broadcasted_iota(jnp.int32, (B, n), 1)
        X[rows, :] = k + jnp.where(ri == ci, jnp.broadcast_to(noise_ref[...], (B, n)), 0.0)
    tri = lax.broadcasted_iota(jnp.int32, (B, B), 0) >= lax.broadcasted_iota(jnp.int32, (B, B), 1)
    eye = jnp.where(lax.broadcasted_iota(jnp.int32, (B, B), 0) == lax.broadcasted_iota(jnp.int32, (B, B), 1), 1.0, 0.0)

    def step(b, _):
        r0 = pl.multiple_of(b * B, B)
        def load(g):
            return X[pl.ds(r0 + 8 * g, 8), pl.ds(r0, B)]
        def store(g, v):
            V[pl.ds(8 * g, 8), :] = v
        factor_block(load, store)
        v = jnp.where(tri, V[...], 0.0)
        X[pl.ds(r0, B), pl.ds(r0, B)] = eye
        P = dot3(split(v), split(X[pl.ds(r0, B), :]))
        X[pl.ds(r0, B), :] = P
        Ps = split(P)
        def upd(i, _):
            i0 = pl.multiple_of(i * B, B)
            T = X[pl.ds(r0, B), pl.ds(i0, B)].T
            X[pl.ds(i0, B), pl.ds(r0, B)] = jnp.zeros((B, B), jnp.float32)
            X[pl.ds(i0, B), :] = X[pl.ds(i0, B), :] - dot3(split(T), Ps)
            return 0
        lax.fori_loop(b + 1, nb, upd, 0)
        return 0
    lax.fori_loop(0, nb, step, 0)
    for i in range(nb):
        rows = slice(i * B, (i + 1) * B)
        ri = lax.broadcasted_iota(jnp.int32, (B, n), 0) + i * B
        ci = lax.broadcasted_iota(jnp.int32, (B, n), 1)
        w = jnp.where(ri >= ci, X[rows, :], 0.0)
        h, lo = split(w)
        w_ref[0, rows, :] = h; w_ref[1, rows, :] = lo
        wt_ref[0, :, rows] = h.T; wt_ref[1, :, rows] = lo.T

def chol_call(zl, noise):
    width, n = zl.shape
    def k(zl_ref, noise_ref, w_ref, wt_ref, X, V, zt):
        chol_body(zl_ref, noise_ref, w_ref, wt_ref, X, V, zt, n, width)
    o = jax.ShapeDtypeStruct((2, n, n), jnp.bfloat16)
    return pl.pallas_call(k, out_shape=(o, o),
        in_specs=[pl.BlockSpec(memory_space=pltpu.VMEM)]*2,
        out_specs=[pl.BlockSpec(memory_space=pltpu.VMEM)]*2,
        scratch_shapes=[pltpu.VMEM((n, n), jnp.float32), pltpu.VMEM((B, B), jnp.float32), pltpu.VMEM((n, width), jnp.bfloat16)],
        compiler_params=pltpu.CompilerParams(vmem_limit_bytes=60*2**20))(zl, noise)

B=128
bf16=jnp.bfloat16; f32=jnp.float32

def main_body(pos_ref, zl_ref, zr_ref, zc_ref, w_ref, wt_ref, nz_ref, out_ref, fac_ref,
              zlt, zrt, kh, kl, lh, ll, gh, gl, g1, hr, hlc, stage, sem, *, width, lead, nrow, ncol, passes, RT=512, CT=256):
    rows = zr_ref.shape[1]; cols = zc_ref.shape[1]
    p = pos_ref[0]; q = pos_ref[1]
    cs = LOG2E / (2 * width)
    for i in range(0, lead, 256):
        zlt[i:i+256, :] = zl_ref[:, i:i+256].T
    def colsq(ref, sl):
        x = ref[:, sl].astype(f32)
        return jnp.sum(x * x, axis=0, keepdims=True) * cs
    def lanecol(v):
        return jnp.broadcast_to(jnp.broadcast_to(v, (8, v.shape[1])).T[:, 0:1], (v.shape[1], B))
    for i in range(0, rows, 256):
        zrt[i:i+256, :] = zr_ref[:, i:i+256].T
        hr[i:i+256, :] = lanecol(colsq(zr_ref, slice(i, i+256)))
    for i in range(0, lead, 256):
        hlc[i:i+256, :] = lanecol(colsq(zl_ref, slice(i, i+256)))
    def wide(x, n):
        return jnp.concatenate([x] * (n // B), axis=1)
    for j in range(0, lead, 256):
        hl = colsq(zl_ref, slice(j, j + 256))
        for i in range(0, rows, RT):
            t = dot(zrt[i:i+RT, :], zl_ref[:, j:j+256]) * (2 * cs) - wide(hr[i:i+RT, :], 256) - hl
            k = jnp.exp2(t)
            if i == 0:
                ri = lax.broadcasted_iota(jnp.int32, (B, 256), 0) + p * B
                ci = lax.broadcasted_iota(jnp.int32, (B, 256), 1) + j
                nug = jnp.where(ri == ci, jnp.broadcast_to(nz_ref[:, j:j+256], (B, 256)), 0.0)
                k = jnp.concatenate([k[:B] + nug, k[B:]], axis=0)
            h, l = split(k)
            kh[i:i+RT, j:j+256] = h
            kl[i:i+RT, j:j+256] = l
    for j in range(0, lead, 256):
        e = j + 256
        for i in range(0, rows, RT):
            rs = slice(i, i + RT)
            x = dot(kh[rs, :e], wt_ref[0, :e, j:e]) + dot(kh[rs, :e], wt_ref[1, :e, j:e]) + dot(kl[rs, :e], wt_ref[0, :e, j:e])
            h, l = split(x)
            lh[rs, j:e] = h
            ll[rs, j:e] = l
            for half in range(2):
                @pl.when(q == j // B + half)
                def _():
                    y = x[:, half * B:(half + 1) * B]
                    if i == 0:
                        ri = lax.broadcasted_iota(jnp.int32, (B, B), 0) + p * B
                        ci = lax.broadcasted_iota(jnp.int32, (B, B), 1) + (j + half * B)
                        y = jnp.concatenate([jnp.where(ri >= ci, y[:B], 0.0), y[B:]], axis=0)
                    fac_ref[rs, :] = y
    for i in range(0, rows, RT):
        rs = slice(i, i + RT)
        tot = None
        for j in range(0, lead, 256):
            x = dot(lh[rs, j:], w_ref[0, j:, j:j+256]) + dot(lh[rs, j:], w_ref[1, j:, j:j+256]) + dot(ll[rs, j:], w_ref[0, j:, j:j+256])
            h, l = split(x)
            gh[rs, j:j+256] = h
            if passes == 3:
                gl[rs, j:j+256] = l
            sm = jnp.sum(x, axis=1, keepdims=True)
            tot = sm if tot is None else tot + sm
        g1[rs, :] = jnp.broadcast_to(tot, (RT, B))
    nch = cols // CT
    bc = CT // B
    def copies(c, slot):
        return [pltpu.make_async_copy(stage.at[slot, :, pl.ds(u * B, B)], out_ref.at[:, c * bc + u, 0, :], sem.at[slot]) for u in range(bc)]
    def chunk(c, _):
        slot = lax.rem(c, 2)
        c0 = pl.multiple_of(c * CT, CT)
        zc = zc_ref[:, pl.ds(c0, CT)]
        x = zc.astype(f32)
        hc = jnp.sum(x * x, axis=0, keepdims=True) * cs
        kc = jnp.exp2(dot(zlt[...], zc) * (2 * cs) - wide(hlc[...], CT) - hc)
        mu = jnp.mean(kc, axis=0, keepdims=True)
        dh, dl = split(kc - mu)
        @pl.when(c >= 2)
        def _():
            for cp in copies(c, slot): cp.wait()
        for i in range(0, rows, RT):
            rs = slice(i, i + RT)
            t = dot(zrt[rs, :], zc) * (2 * cs) - wide(hr[rs, :], CT) - hc
            k = jnp.exp2(t)
            s = dot(gh[rs, :], dh)
            if passes == 3:
                s = s + dot(gh[rs, :], dl) + dot(gl[rs, :], dh)
            k = k - s - wide(g1[rs, :], CT) * mu
            stage[slot, rs, :] = k
        for u in range(bc):
            gb = (c * bc + u) * ncol + q
            a = gb // nrow
            @pl.when((gb % nrow == p))
            def _():
                r0 = pl.multiple_of(a * B, B)
                ri = lax.broadcasted_iota(jnp.int32, (B, B), 0)
                ci = lax.broadcasted_iota(jnp.int32, (B, B), 1)
                nzv = nz_ref[:, pl.ds(pl.multiple_of(gb * B, B), B)]
                stage[slot, pl.ds(r0, B), u*B:(u+1)*B] = stage[slot, pl.ds(r0, B), u*B:(u+1)*B] + jnp.where(ri == ci, jnp.broadcast_to(nzv, (B, B)), 0.0)
            @pl.when(gb * B < lead)
            def _():
                stage[slot, :, u*B:(u+1)*B] = jnp.zeros((rows, B), f32)
        @pl.when(p * B < lead)
        def _():
            stage[slot, :B, :] = jnp.zeros((B, CT), f32)
        for cp in copies(c, slot): cp.start()
        return 0
    lax.fori_loop(0, nch, chunk, 0)
    for c in (nch - 2, nch - 1):
        for cp in copies(c, c % 2): cp.wait()

def main_call(pos, zl, zr, zc, w, wt, nz, nrow=16, ncol=8, passes=3):
    width, lead = zl.shape; rows = zr.shape[1]; cols = zc.shape[1]
    V = pl.BlockSpec(memory_space=pltpu.VMEM)
    return pl.pallas_call(functools.partial(main_body, width=width, lead=lead, nrow=nrow, ncol=ncol, passes=passes),
        out_shape=(jax.ShapeDtypeStruct((rows, cols // B, 1, B), f32), jax.ShapeDtypeStruct((rows, B), f32)),
        in_specs=[pl.BlockSpec(memory_space=pltpu.SMEM)] + [V] * 6,
        out_specs=(pl.BlockSpec(memory_space=pltpu.HBM), V),
        scratch_shapes=[pltpu.VMEM((lead, width), bf16), pltpu.VMEM((rows, width), bf16)] +
          [pltpu.VMEM((rows, lead), bf16)] * 6 + [pltpu.VMEM((rows, B), f32)] * 2 + [pltpu.VMEM((lead, B), f32),
          pltpu.VMEM((2, rows, 256), f32), pltpu.SemaphoreType.DMA((2,))],
        compiler_params=pltpu.CompilerParams(vmem_limit_bytes=61*2**20),
    )(pos, zl, zr, zc, w, wt, nz)


def body(embeddings, inv_scale, noise):
    nrow = lax.axis_size("row")
    ncol = lax.axis_size("col")
    prow = lax.axis_index("row")
    qcol = lax.axis_index("col")
    total, fdev = embeddings.shape
    width = inv_scale.shape[0]
    crow = total // (TILE * nrow)
    ccol = total // (TILE * ncol)
    lead = PANELS * PB
    scale_part = lax.dynamic_slice_in_dim(inv_scale, (prow * ncol + qcol) * fdev, fdev)
    scaled = (embeddings.T.astype(jnp.float32) * scale_part[:, None]).astype(jnp.bfloat16)
    zl = lax.all_gather(scaled[:, :lead], ("row", "col"), axis=0, tiled=True)
    by_row = scaled.reshape(fdev, crow, nrow, TILE).transpose(2, 0, 1, 3).reshape(nrow, fdev, crow * TILE)
    by_col = scaled.reshape(fdev, ccol, ncol, TILE).transpose(2, 0, 1, 3).reshape(ncol, fdev, ccol * TILE)
    col_mine = lax.all_to_all(by_col, "col", split_axis=0, concat_axis=0, tiled=True)
    row_mine = lax.all_to_all(by_row, "row", split_axis=0, concat_axis=0, tiled=True)
    zc = lax.all_gather(col_mine, "row", axis=0, tiled=False).reshape(width, ccol * TILE)
    zr = lax.all_gather(row_mine, "col", axis=0, tiled=False).transpose(1, 0, 2, 3).reshape(width, crow * TILE)
    nz = noise[None]
    w, wt = chol_call(zl, nz[:, :lead])
    pos = jnp.stack([prow, qcol]).astype(jnp.int32)
    schur, factor = main_call(pos, zl, zr, zc, w, wt, nz, nrow=nrow, ncol=ncol, passes=3)
    return (
        factor.reshape(crow, 1, TILE, TILE),
        schur.reshape(crow, 1, TILE, ccol, 1, TILE),
    )


def solution(mesh):
    placed = (P(None, ("row", "col")), P(), P())
    return jax.shard_map(
        body,
        mesh=mesh,
        in_specs=placed,
        out_specs=(P(None, "row", None, "col"), P(None, "row", None, None, "col", None)),
        check_vma=False,
    )
```

time: 1290 us -> 278 us (0.22)
  waiting for transfers between devices: 591 us -> 48.5 us
  other arithmetic: 285 us -> 2.9 us
  matrix products: 183 us -> 0 us
  Pallas kernels: 0 us -> 174 us
  local copies, waits for them, and re-layouts: 163 us -> 6.69 us
    psum x6 -> x0, waiting for transfers between devices: 545 us -> none  [the longest x2 243 us: from_root(): return lax.psum(jnp.where(mine, shard, jnp.zeros_like(shard)), axis)]
    another operation x36 -> x1, other arithmetic: 246 us -> 0.64 us  [body(): pos = jnp.stack([prow, qcol]).astype(jnp.int32)]
    pallas_call x0 -> x2, Pallas kernels: none -> 174 us  [the longest x1 100 us: main_call(): pl.pallas_call(functools.partial(main_body, width=width, lead=lead, nrow=...]
    dot_general x3 -> x0, matrix products: 151 us -> none  [the longest x2 135 us: trailing_update(): lax.dot_general(left_rows, right_rows, (((1,), (1,)), ((), ())), precisio...]
    unnamed x39 -> x0, local copies, waits for them, and re-layouts: 33.4 us -> none
    another operation x26 -> x0, matrix products: 31.9 us -> none  [the longest x14 24.5 us: body(): left_rows = jax.scipy.linalg.solve_triangular(chol, panel.T, lower=True).T]
    another operation x37 -> x0, local copies, waits for them, and re-layouts: 21.1 us -> none  [the longest x27 18.8 us: body(): left_rows = jax.scipy.linalg.solve_triangular(chol, panel.T, lower=True).T]
    sub x1 -> x0, local copies, waits for them, and re-layouts: 18.7 us -> none  [body(): matrix = matrix - trailing_update(left_rows, right_rows)]
  transfers between devices with their start and end apart: 8 -> 3, of which waited for: 7 -> 2; matrix products, arithmetic and copies ran while one was open for 4% -> 3% of each run, Pallas kernels for 0% -> 27%
where the time goes in v1:
time: 278 us
  Pallas kernels  174 us (63%)
  waiting for transfers between devices  48.5 us (17%)
  blocking collectives  31.9 us (11%)
  between operations  13.8 us (5%)
  local copies, waits for them, and re-layouts  6.69 us (2%)
  other arithmetic  2.9 us (1%)
    pallas_call x1, Pallas kernels, main_call(): pl.pallas_call(functools.partial(main_body, width=width, lead=lead, nrow=...  100 us
    pallas_call x1, Pallas kernels, chol_call(): pl.pallas_call(k, out_shape=(o, o), in_specs=[pl.BlockSpec(memory_space=p...  73.9 us
    all_gather x1, waiting for transfers between devices, body(): zl = lax.all_gather(scaled[:, :lead], ('row', 'col'), axis=0, tiled=True)  36.2 us
    all_to_all x1, blocking collectives, body(): lax.all_to_all(by_row, 'row', split_axis=0, concat_axis=0, tiled=True)  16.7 us
    all_to_all x1, blocking collectives, body(): lax.all_to_all(by_col, 'col', split_axis=0, concat_axis=0, tiled=True)  15.2 us
    all_gather x1, waiting for transfers between devices, body(): lax.all_gather(col_mine, 'row', axis=0, tiled=False)  12.2 us
  transfers between devices with their start and end apart: 3, of which 2 were waited for; matrix products, arithmetic and copies ran while one was open for 3% of the time, Pallas kernels for 27%

profile of v1, /device:TPU:1, one launch (start us, length us, event | category | flops | bytes accessed | tf_op | source)
XLA Modules:
  0.0 278.1 jit_solution(13651286824142440553)
XLA Ops:
  7.2 0.0 all-gather.6.cloned.1.call-start
  7.2 0.8 dynamic_slice.3
  8.0 1.1 fusion
  9.1 0.6 slice.8
  9.7 0.0 all-gather.6.cloned.1.call-update
  9.7 0.0 all-gather.8.cloned.1.call-start
  9.8 1.1 multiply_convert_fusion
  10.9 0.1 copy.21
  11.0 16.7 %all_to_all.10 = bf16[16,8,1536]{2,1,0:T(8,128)(2,1)} all-to-all(bf16[16,8,1536]{2,1,0:T(8,128)(2,1)S(1)} %bitcast.36), channel_id=1, replica_groups=mesh['row'=16,'col'=8] {'row'}, dimensions={0} | all-to-all | bytes 786432 | tf_op jit(solution)/shard_map/all_to_all | solution.py:270
  27.7 0.0 all-gather.8.cloned.1.call-update
  27.7 0.0 all-gather.10.cloned.1.call-start
  27.7 0.1 copy.20
  27.8 15.2 %all_to_all.11 = bf16[8,8,3072]{2,1,0:T(8,128)(2,1)} all-to-all(bf16[8,8,3072]{2,1,0:T(8,128)(2,1)S(1)} %bitcast.35), channel_id=1, replica_groups=mesh['row'=16,'col'=8] {'col'}, dimensions={0} | all-to-all | bytes 786432 | tf_op jit(solution)/shard_map/all_to_all | solution.py:269
  43.0 0.0 all-gather.10.cloned.1.call-update
  43.1 1.3 slice.9.noise_ref
  44.3 0.6 pad_add_fusion.pos_ref
  45.0 36.2 %all-gather.6.cloned.1.call-done.zl_ref = bf16[1024,1024]{1,0:T(8,128)(2,1)} async-done(((bf16[8,1024]{1,0:T(8,128)(2,1)}), bf16[1024,1024]{1,0:T(8,128)(2,1)}) %all-gather.6.cloned.1.call-update) | async-done | bytes 2097168 | tf_op jit(solution)/shard_map/all_gather | solution.py:266
  81.2 73.9 %shard_map.50 = (bf16[2,1024,1024]{2,1,0:T(8,128)(2,1)}, bf16[2,1024,1024]{2,1,0:T(8,128)(2,1)}) custom-call(bf16[1024,1024]{1,0:T(8,128)(2,1)} %all-gather.6.cloned.1.call-done.zl_ref, f32[1,1024]{1,0:T(1,128)} %slice.9.noise_ref), custom_call_target="tpu_custom_call" | custom-call | tf_op jit(solution)/shard_map/pallas_call | solution.py:123
  155.1 0.0 all-gather.8.cloned.1.call-done
  155.1 3.9 %copy.14 = bf16[16,8,8,1536]{3,2,1,0:T(8,128)(2,1)} copy(bf16[16,8,8,1536]{3,2,0,1:T(8,128)(2,1)} %bitcast.34) | data formatting | bytes 6291456 | tf_op jit(solution)/shard_map/transpose | solution.py:272
  159.0 12.2 %all-gather.10.cloned.1.call-done = bf16[128,8,3072]{2,1,0:T(8,128)(2,1)} async-done(((bf16[8,8,3072]{2,1,0:T(8,128)(2,1)}), bf16[128,8,3072]{2,1,0:T(8,128)(2,1)}) %all-gather.10.cloned.1.call-update) | async-done | bytes 6291472 | tf_op jit(solution)/shard_map/all_gather | solution.py:271
  171.2 100.4 %shard_map.51 = (f32[1536,24,1,128]{3,2,1,0:T(1,128)}, f32[1536,128]{1,0:T(8,128)}) custom-call(s32[2]{0:T(128)} %pad_add_fusion.pos_ref, bf16[1024,1024]{1,0:T(8,128)(2,1)} %all-gather.6.cloned.1.call-done.zl_ref, bf16[1024,1536]{1,0:T(8,128)(2,1)} %bitcast.30, bf16[1024,3072]{1,0:T(8,128)(2,1)} %bitcast.31, bf16[2,1024,1024]{2,1,0:T(8,128)(2,1)} %get-tuple-element.6.w_ref, ...), custom_call_target="tpu_custom_call" | custom-call | tf_op jit(solution)/shard_map/pallas_call | solution.py:243
Async XLA Ops:
  7.2 74.0 %all-gather.6.cloned.1.call-start = ((), (), s32[]{:S(2)}) async-start(), calls=%async_computation.2 | async-start | bytes 2113536 | tf_op jit(solution)/shard_map/all_gather | solution.py:266
  9.7 145.3 %all-gather.8.cloned.1.call-start = ((), (), s32[]{:S(2)}) async-start(), calls=%async_computation.3 | async-start | bytes 3538944 | tf_op jit(solution)/shard_map/all_gather | solution.py:272
  27.7 143.5 %all-gather.10.cloned.1.call-start = ((), (), s32[]{:S(2)}) async-start(), calls=%async_computation.4 | async-start | bytes 6684672 | tf_op jit(solution)/shard_map/all_gather | solution.py:271
Sparse Core Ops, SparseCore 0:
  11.7 69.4 all-gather.5
  82.9 25.4 all-gather.7
  110.5 60.6 all-gather.9

commit v2 on v1

--- a/solution.py
+++ b/solution.py
@@ -11,6 +11,7 @@
 TILE = 128
 PB = 512
 PANELS = 2
+PASSES = 3
 B=128
 def factor_block(load, store):
     lane = lax.broadcasted_iota(jnp.int32, (8, B), 1)
@@ -69,7 +70,7 @@
 
 LOG2E = math.log2(math.e)
 
-def chol_body(zl_ref, noise_ref, w_ref, wt_ref, X, V, zt, n, width):
+def chol_body(zl_ref, noise_ref, w_ref, wt_ref, X, V, zt, n, width, poll=None):
     nb = n // B
     zt[...] = zl_ref[...].T
     zf = zl_ref[...].astype(jnp.float32)
@@ -86,6 +87,8 @@
     eye = jnp.where(lax.broadcasted_iota(jnp.int32, (B, B), 0) == lax.broadcasted_iota(jnp.int32, (B, B), 1), 1.0, 0.0)
 
     def step(b, _):
+        if poll is not None:
+            poll(b)
         r0 = pl.multiple_of(b * B, B)
         def load(g):
             return X[pl.ds(r0 + 8 * g, 8), pl.ds(r0, B)]
@@ -115,23 +118,265 @@
         w_ref[0, rows, :] = h; w_ref[1, rows, :] = lo
         wt_ref[0, :, rows] = h.T; wt_ref[1, :, rows] = lo.T
 
-def chol_call(zl, noise):
-    width, n = zl.shape
-    def k(zl_ref, noise_ref, w_ref, wt_ref, X, V, zt):
-        chol_body(zl_ref, noise_ref, w_ref, wt_ref, X, V, zt, n, width)
-    o = jax.ShapeDtypeStruct((2, n, n), jnp.bfloat16)
-    return pl.pallas_call(k, out_shape=(o, o),
-        in_specs=[pl.BlockSpec(memory_space=pltpu.VMEM)]*2,
-        out_specs=[pl.BlockSpec(memory_space=pltpu.VMEM)]*2,
-        scratch_shapes=[pltpu.VMEM((n, n), jnp.float32), pltpu.VMEM((B, B), jnp.float32), pltpu.VMEM((n, width), jnp.bfloat16)],
-        compiler_params=pltpu.CompilerParams(vmem_limit_bytes=60*2**20))(zl, noise)
 
 B=128
 bf16=jnp.bfloat16; f32=jnp.float32
 
+MESH = pl.DeviceIdType.MESH
+HALF = 768
+
+
+def lead_kernel(slab_ref, scale_ref, noise_ref, zl_out, zr_ref, zc_ref, w_ref, wt_ref,
+                xs, xr, s16, zlb, zlo, X, V, zt, own_sem, ssem, rsem, *, width, lead, half):
+    p = lax.axis_index("row")
+    qq = lax.axis_index("col")
+    z = qq // 2
+    c = qq % 2
+    y = p // 4
+    x = p % 4
+    k16 = pl.multiple_of((p * 4 + z) * 16, 16)
+    nh = 16 * half
+
+    def dev(pp, zz, cc):
+        return (pp, zz * 2 + cc)
+
+    def rot(v, d):
+        return (v + d + 4) % 4
+
+    def plane(dy, dx):
+        return rot(y, dy) * 4 + rot(x, dx)
+
+    plane_offsets = [(dy, dx) for dy in range(4) for dx in range(4) if (dy, dx) != (0, 0)]
+    col_offsets = [(dz, dc) for dz in range(4) for dc in range(2) if (dz, dc) != (0, 0)]
+
+    barrier = pltpu.get_barrier_semaphore()
+    for dy, dx in plane_offsets:
+        pl.semaphore_signal(barrier, inc=1, device_id=dev(plane(dy, dx), z, c), device_id_type=MESH)
+    for dz, dc in col_offsets:
+        pl.semaphore_signal(barrier, inc=1, device_id=dev(p, rot(z, dz), (c + dc) % 2), device_id_type=MESH)
+
+    def remote(src, dst, i, target):
+        return pltpu.make_async_remote_copy(src_ref=src, dst_ref=dst, send_sem=ssem.at[i], recv_sem=rsem.at[i],
+                                            device_id=target, device_id_type=MESH)
+
+    def step_a(pp, d):
+        yy, xx = pp // 4, pp % 4
+        return (yy * 4 + rot(xx, d)) * (1 - c) + (rot(yy, d) * 4 + xx) * c
+
+    def step_b(pp, d):
+        yy, xx = pp // 4, pp % 4
+        return (yy * 4 + rot(xx, d)) * c + (rot(yy, d) * 4 + xx) * (1 - c)
+
+    def block(pp):
+        return pl.ds(pl.multiple_of(pp * 64, 64), 64)
+
+    base = {}
+    at = 0
+    for name, n in (("X", 1), ("L1", 3), ("L2", 15), ("L3", 1), ("CA", 7), ("RA", 15), ("A1", 2), ("A2", 2),
+                    ("B1", 8), ("B2", 8), ("Z1", 2), ("Z2", 2), ("PR", 1)):
+        base[name] = at
+        at += n
+    DS = (0, 1, -1, 2)
+
+    def exchange():
+        return [remote(xs, xr, base["X"], dev(p, z, 1 - c))]
+
+    def lead_z():
+        r = zlb.at[c, pl.ds(k16, 16), :]
+        return [remote(r, r, base["L1"] + d - 1, dev(p, rot(z, d), c)) for d in (1, 2, 3)]
+
+    def lead_plane():
+        r = zlb.at[c, block(p), :]
+        return [remote(r, r, base["L2"] + n, dev(plane(dy, dx), z, c)) for n, (dy, dx) in enumerate(plane_offsets)]
+
+    def lead_partner():
+        r = zlb.at[c]
+        return [remote(r, r, base["L3"], dev(p, z, 1 - c))]
+
+    def col_a2a():
+        out = []
+        for n, (dz, dc) in enumerate(col_offsets):
+            zz, cc = rot(z, dz), (c + dc) % 2
+            out.append(remote(s16.at[:, zz * 2 + cc], zc_ref.at[:, c, pl.ds(k16, 16), :], base["CA"] + n, dev(p, zz, cc)))
+        return out
+
+    def row_a2a():
+        out = []
+        for n, (dy, dx) in enumerate(plane_offsets):
+            pp = plane(dy, dx)
+            out.append(remote(s16.at[pp // 8, pp % 8], zr_ref.at[c, p, z], base["RA"] + n, dev(pp, z, c)))
+        return out
+
+    def own_copies():
+        return [pltpu.make_async_copy(s16.at[:, qq], zc_ref.at[:, c, pl.ds(k16, 16), :], own_sem.at[0]),
+                pltpu.make_async_copy(s16.at[p // 8, p % 8], zr_ref.at[c, p, z], own_sem.at[1])]
+
+    def a1():
+        r = zc_ref.at[:, :, block(p), :]
+        return [remote(r, r, base["A1"], dev(step_a(p, 1), z, c)), remote(r, r, base["A1"] + 1, dev(step_a(p, -1), z, c))]
+
+    def a2():
+        f = zc_ref.at[0, :, block(step_a(p, -1)), :]
+        g = zc_ref.at[1, :, block(step_a(p, 1)), :]
+        return [remote(f, f, base["A2"], dev(step_a(p, 1), z, c)), remote(g, g, base["A2"] + 1, dev(step_a(p, -1), z, c))]
+
+    def b1(n):
+        r = zc_ref.at[:, :, block(step_a(p, DS[n])), :]
+        return [remote(r, r, base["B1"] + 2 * n, dev(step_b(p, 1), z, c)),
+                remote(r, r, base["B1"] + 2 * n + 1, dev(step_b(p, -1), z, c))]
+
+    def b2(n):
+        f = zc_ref.at[0, :, block(step_a(step_b(p, -1), DS[n])), :]
+        g = zc_ref.at[1, :, block(step_a(step_b(p, 1), DS[n])), :]
+        return [remote(f, f, base["B2"] + 2 * n, dev(step_b(p, 1), z, c)),
+                remote(g, g, base["B2"] + 2 * n + 1, dev(step_b(p, -1), z, c))]
+
+    def z1():
+        r = zr_ref.at[c, :, z]
+        return [remote(r, r, base["Z1"], dev(p, rot(z, 1), c)), remote(r, r, base["Z1"] + 1, dev(p, rot(z, -1), c))]
+
+    def z2():
+        f = zr_ref.at[c, 0:8, rot(z, -1)]
+        g = zr_ref.at[c, 8:16, rot(z, 1)]
+        return [remote(f, f, base["Z2"], dev(p, rot(z, 1), c)), remote(g, g, base["Z2"] + 1, dev(p, rot(z, -1), c))]
+
+    def partner_rows():
+        r = zr_ref.at[c]
+        return [remote(r, r, base["PR"], dev(p, z, 1 - c))]
+
+    def start(copies):
+        for cp in copies:
+            cp.start()
+
+    def arrived(copies):
+        for cp in copies:
+            cp.wait_recv()
+
+    scale = scale_ref[:, 0:1]
+
+    def scaled(sl):
+        return (slab_ref[:, sl].astype(f32) * scale).astype(bf16).astype(f32)
+
+    CH = 2048
+    for h in range(2):
+        @pl.when(c == 1 - h)
+        def _():
+            for o in range(0, nh, CH):
+                xs[:, o:o + CH] = scaled(slice(h * nh + o, h * nh + o + CH))
+    xs[:, nh:] = scaled(slice(0, lead))
+    pl.semaphore_wait(barrier, len(plane_offsets) + len(col_offsets))
+    start(exchange())
+    arrived(exchange())
+
+    def pair(own, other):
+        first = own * (1 - c).astype(f32) + other * c.astype(f32)
+        second = other * (1 - c).astype(f32) + own * c.astype(f32)
+        return jnp.concatenate([first, second], axis=0).astype(bf16)
+
+    for j in range(lead // B // 2):
+        for h in range(2):
+            @pl.when(c == h)
+            def _():
+                o = (2 * j + h) * B
+                zlb[h, pl.ds(k16, 16), j * B:(j + 1) * B] = pair(xs[:, nh + o:nh + o + B], xr[:, nh + o:nh + o + B])
+    start(lead_z())
+    for h in range(2):
+        @pl.when(c == h)
+        def _():
+            for a in range(half // B):
+                own = scaled(slice(h * nh + a * 2048, h * nh + (a + 1) * 2048))
+                both = pair(own, xr[:, a * 2048:(a + 1) * 2048])
+                for s in range(16):
+                    s16[s // 8, s % 8, :, a * B:(a + 1) * B] = both[:, s * B:(s + 1) * B]
+    arrived(lead_z())
+    start(lead_plane())
+    arrived(lead_plane())
+    start(lead_partner())
+    start(col_a2a())
+    start(own_copies())
+    start(row_a2a())
+    arrived(lead_partner())
+
+    for u in range(lead // B):
+        zlo[:, u * B:(u + 1) * B] = zlb[u % 2, :, (u // 2) * B:(u // 2 + 1) * B]
+    zl_copy = pltpu.make_async_copy(zlo, zl_out, own_sem.at[2])
+    zl_copy.start()
+
+    def poll(b):
+        @pl.when(b == 0)
+        def _():
+            for cp in own_copies():
+                cp.wait()
+            arrived(col_a2a())
+            start(a1())
+            arrived(row_a2a())
+            start(z1())
+
+        @pl.when(b == 1)
+        def _():
+            start(b1(0))
+            arrived(a1())
+            start(a2())
+            start(b1(1))
+            start(b1(2))
+            arrived(z1())
+            start(z2())
+
+        @pl.when(b == 2)
+        def _():
+            arrived(a2())
+            start(b1(3))
+            arrived(z2())
+            start(partner_rows())
+
+        @pl.when(b == 3)
+        def _():
+            arrived(b1(0))
+            start(b2(0))
+
+        @pl.when(b == 4)
+        def _():
+            for n in (1, 2, 3):
+                arrived(b1(n))
+                start(b2(n))
+
+    chol_body(zlo, noise_ref, w_ref, wt_ref, X, V, zt, lead, width, poll)
+    for n in range(4):
+        arrived(b2(n))
+    arrived(partner_rows())
+    zl_copy.wait()
+    sent = exchange() + lead_z() + lead_plane() + lead_partner() + col_a2a() + row_a2a() + a1() + a2() + z1() + z2() + partner_rows()
+    for n in range(4):
+        sent += b1(n) + b2(n)
+    for cp in sent:
+        cp.wait_send()
+
+
+def lead_call(slab, scale, noise, lead, width):
+    total = slab.shape[1]
+    half = total // 32
+    o = jax.ShapeDtypeStruct((2, lead, lead), bf16)
+    vm = pl.BlockSpec(memory_space=pltpu.VMEM)
+    hbm = pl.BlockSpec(memory_space=pltpu.HBM)
+    nsem = 67
+    return pl.pallas_call(
+        functools.partial(lead_kernel, width=width, lead=lead, half=half),
+        out_shape=(jax.ShapeDtypeStruct((width, lead), bf16), jax.ShapeDtypeStruct((2, 16, 4, 16, half), bf16),
+                   jax.ShapeDtypeStruct((2, 2, width, half), bf16), o, o),
+        in_specs=[vm] * 3,
+        out_specs=[hbm, hbm, hbm, vm, vm],
+        scratch_shapes=[pltpu.VMEM((8, 16 * half + lead), f32), pltpu.VMEM((8, 16 * half + lead), f32),
+                        pltpu.VMEM((2, 8, 16, half), bf16), pltpu.VMEM((2, width, lead // 2), bf16),
+                        pltpu.VMEM((width, lead), bf16), pltpu.VMEM((lead, lead), f32), pltpu.VMEM((B, B), f32),
+                        pltpu.VMEM((lead, width), bf16), pltpu.SemaphoreType.DMA((3,)),
+                        pltpu.SemaphoreType.DMA((nsem,)), pltpu.SemaphoreType.DMA((nsem,))],
+        compiler_params=pltpu.CompilerParams(vmem_limit_bytes=60 * 2**20, collective_id=0, has_side_effects=True),
+    )(slab, scale, noise)
+
+
 def main_body(pos_ref, zl_ref, zr_ref, zc_ref, w_ref, wt_ref, nz_ref, out_ref, fac_ref,
               zlt, zrt, kh, kl, lh, ll, gh, gl, g1, hr, hlc, stage, sem, *, width, lead, nrow, ncol, passes, RT=512, CT=256):
-    rows = zr_ref.shape[1]; cols = zc_ref.shape[1]
+    half = zr_ref.shape[2]; rows = 2 * half
     p = pos_ref[0]; q = pos_ref[1]
     cs = LOG2E / (2 * width)
     for i in range(0, lead, 256):
@@ -142,8 +387,10 @@
     def lanecol(v):
         return jnp.broadcast_to(jnp.broadcast_to(v, (8, v.shape[1])).T[:, 0:1], (v.shape[1], B))
     for i in range(0, rows, 256):
-        zrt[i:i+256, :] = zr_ref[:, i:i+256].T
-        hr[i:i+256, :] = lanecol(colsq(zr_ref, slice(i, i+256)))
+        part = zr_ref.at[i // half]
+        o = i % half
+        zrt[i:i+256, :] = part[:, o:o+256].T
+        hr[i:i+256, :] = lanecol(colsq(part, slice(o, o+256)))
     for i in range(0, lead, 256):
         hlc[i:i+256, :] = lanecol(colsq(zl_ref, slice(i, i+256)))
     def wide(x, n):
@@ -169,13 +416,13 @@
             h, l = split(x)
             lh[rs, j:e] = h
             ll[rs, j:e] = l
-            for half in range(2):
-                @pl.when(q == j // B + half)
+            for hb in range(2):
+                @pl.when(q == j // B + hb)
                 def _():
-                    y = x[:, half * B:(half + 1) * B]
+                    y = x[:, hb * B:(hb + 1) * B]
                     if i == 0:
                         ri = lax.broadcasted_iota(jnp.int32, (B, B), 0) + p * B
-                        ci = lax.broadcasted_iota(jnp.int32, (B, B), 1) + (j + half * B)
+                        ci = lax.broadcasted_iota(jnp.int32, (B, B), 1) + (j + hb * B)
                         y = jnp.concatenate([jnp.where(ri >= ci, y[:B], 0.0), y[B:]], axis=0)
                     fac_ref[rs, :] = y
     for i in range(0, rows, RT):
@@ -190,14 +437,18 @@
             sm = jnp.sum(x, axis=1, keepdims=True)
             tot = sm if tot is None else tot + sm
         g1[rs, :] = jnp.broadcast_to(tot, (RT, B))
-    nch = cols // CT
+    nch = 4 * half // CT
     bc = CT // B
+    per = half // CT
+    def col_block(c, u):
+        g = c // per
+        return 2 * ((g % 2) * (half // B) + (c % per) * bc + u) + g // 2
     def copies(c, slot):
-        return [pltpu.make_async_copy(stage.at[slot, :, pl.ds(u * B, B)], out_ref.at[:, c * bc + u, 0, :], sem.at[slot]) for u in range(bc)]
+        return [pltpu.make_async_copy(stage.at[slot, :, pl.ds(u * B, B)], out_ref.at[:, col_block(c, u), 0, :], sem.at[slot]) for u in range(bc)]
     def chunk(c, _):
         slot = lax.rem(c, 2)
-        c0 = pl.multiple_of(c * CT, CT)
-        zc = zc_ref[:, pl.ds(c0, CT)]
+        c0 = pl.multiple_of((c % per) * CT, CT)
+        zc = zc_ref[c // per, :, pl.ds(c0, CT)]
         x = zc.astype(f32)
         hc = jnp.sum(x * x, axis=0, keepdims=True) * cs
         kc = jnp.exp2(dot(zlt[...], zc) * (2 * cs) - wide(hlc[...], CT) - hc)
@@ -216,7 +467,7 @@
             k = k - s - wide(g1[rs, :], CT) * mu
             stage[slot, rs, :] = k
         for u in range(bc):
-            gb = (c * bc + u) * ncol + q
+            gb = col_block(c, u) * ncol + q
             a = gb // nrow
             @pl.when((gb % nrow == p))
             def _():
@@ -238,7 +489,7 @@
         for cp in copies(c, c % 2): cp.wait()
 
 def main_call(pos, zl, zr, zc, w, wt, nz, nrow=16, ncol=8, passes=3):
-    width, lead = zl.shape; rows = zr.shape[1]; cols = zc.shape[1]
+    width, lead = zl.shape; rows = 2 * zr.shape[2]; cols = 4 * zc.shape[2]
     V = pl.BlockSpec(memory_space=pltpu.VMEM)
     return pl.pallas_call(functools.partial(main_body, width=width, lead=lead, nrow=nrow, ncol=ncol, passes=passes),
         out_shape=(jax.ShapeDtypeStruct((rows, cols // B, 1, B), f32), jax.ShapeDtypeStruct((rows, B), f32)),
@@ -262,18 +513,13 @@
     ccol = total // (TILE * ncol)
     lead = PANELS * PB
     scale_part = lax.dynamic_slice_in_dim(inv_scale, (prow * ncol + qcol) * fdev, fdev)
-    scaled = (embeddings.T.astype(jnp.float32) * scale_part[:, None]).astype(jnp.bfloat16)
-    zl = lax.all_gather(scaled[:, :lead], ("row", "col"), axis=0, tiled=True)
-    by_row = scaled.reshape(fdev, crow, nrow, TILE).transpose(2, 0, 1, 3).reshape(nrow, fdev, crow * TILE)
-    by_col = scaled.reshape(fdev, ccol, ncol, TILE).transpose(2, 0, 1, 3).reshape(ncol, fdev, ccol * TILE)
-    col_mine = lax.all_to_all(by_col, "col", split_axis=0, concat_axis=0, tiled=True)
-    row_mine = lax.all_to_all(by_row, "row", split_axis=0, concat_axis=0, tiled=True)
-    zc = lax.all_gather(col_mine, "row", axis=0, tiled=False).reshape(width, ccol * TILE)
-    zr = lax.all_gather(row_mine, "col", axis=0, tiled=False).transpose(1, 0, 2, 3).reshape(width, crow * TILE)
+    scale = jnp.broadcast_to(scale_part[:, None], (fdev, TILE))
     nz = noise[None]
-    w, wt = chol_call(zl, nz[:, :lead])
+    zl, zr, zc, w, wt = lead_call(embeddings.T, scale, nz[:, :lead], lead, width)
+    half = zr.shape[-1]
     pos = jnp.stack([prow, qcol]).astype(jnp.int32)
-    schur, factor = main_call(pos, zl, zr, zc, w, wt, nz, nrow=nrow, ncol=ncol, passes=3)
+    schur, factor = main_call(pos, zl, zr.reshape(2, width, half), zc.reshape(4, width, half), w, wt, nz,
+                              nrow=nrow, ncol=ncol, passes=PASSES)
     return (
         factor.reshape(crow, 1, TILE, TILE),
         schur.reshape(crow, 1, TILE, ccol, 1, TILE),

time: 278 us -> 215 us (0.77)
  waiting for transfers between devices: 48.5 us -> 0 us
  Pallas kernels: 174 us -> 210 us
  blocking collectives: 31.9 us -> 0 us
  between operations: 13.8 us -> 0.85 us
  local copies, waits for them, and re-layouts: 6.69 us -> 2.7 us
    all_gather x3 -> x0, waiting for transfers between devices: 48.4 us -> none  [the longest x1 36.2 us: body(): zl = lax.all_gather(scaled[:, :lead], ('row', 'col'), axis=0, tiled=True)]
    pallas_call x1, Pallas kernels: 73.9 us -> 109 us  [lead_call(): pl.pallas_call(functools.partial(lead_kernel, width=width, lead=lead, hal...]
    all_to_all x2 -> x0, blocking collectives: 31.9 us -> none  [the longest x1 16.7 us: body(): lax.all_to_all(by_row, 'row', split_axis=0, concat_axis=0, tiled=True)]
    transpose x2 -> x0, local copies, waits for them, and re-layouts: 3.96 us -> none  [the longest x1 3.89 us: body(): lax.all_gather(row_mine, 'col', axis=0, tiled=False).transpose(1, 0, 2, 3)]
  transfers between devices with their start and end apart: 3 -> 0, of which waited for: 2 -> 0; matrix products, arithmetic and copies ran while one was open for 3% -> 0% of each run, Pallas kernels for 27% -> 0%
where the time goes in v2:
time: 215 us; the launch traced here: 214 us
  Pallas kernels  210 us (98%)
  local copies, waits for them, and re-layouts  2.7 us (1%)
    pallas_call x1, Pallas kernels, lead_call(): pl.pallas_call(functools.partial(lead_kernel, width=width, lead=lead, hal...  109 us
    pallas_call x1, Pallas kernels, main_call(): pl.pallas_call(functools.partial(main_body, width=width, lead=lead, nrow=...  101 us

profile of v2, /device:TPU:1, one launch (start us, length us, event | category | flops | bytes accessed | tf_op | source)
XLA Modules:
  0.0 214.3 jit_solution(18004205515629761214)
XLA Ops:
  0.6 0.6 pad_add_fusion.pos_ref
  1.2 0.8 dynamic_slice.3
  2.0 0.7 broadcast_in_dim.4.scale_ref
  2.6 1.3 slice.4.noise_ref
  3.9 109.4 %shard_map.50 = (bf16[1024,1024]{1,0:T(8,128)(2,1)}, bf16[2,16,4,16,768]{4,3,2,1,0:T(8,128)(2,1)}, bf16[2,2,1024,768]{3,2,1,0:T(8,128)(2,1)}, bf16[2,1024,1024]{2,1,0:T(8,128)(2,1)}, bf16[2,1024,1024]{2,1,0:T(8,128)(2,1)}) custom-call(bf16[8,24576]{1,0:T(8,128)(2,1)} %bitcast.14, f32[8,128]{1,0:T(8,128)} %broadcast_in_dim.4.scale_ref, f32[1,1024]{1,0:T(1,128)} %slice.4.noise_ref), custom_call_target="tpu_custom_call" | custom-call | tf_op jit(solution)/shard_map/pallas_call | solution.py:362
  113.3 100.8 %shard_map.51 = (f32[1536,24,1,128]{3,2,1,0:T(1,128)}, f32[1536,128]{1,0:T(8,128)}) custom-call(s32[2]{0:T(128)} %pad_add_fusion.pos_ref, bf16[1024,1024]{1,0:T(8,128)(2,1)} %get-tuple-element.9.zl_ref, bf16[2,1024,768]{2,1,0:T(8,128)(2,1)} %bitcast.13, bf16[4,1024,768]{2,1,0:T(8,128)(2,1)} %bitcast.12, bf16[2,1024,1024]{2,1,0:T(8,128)(2,1)} %get-tuple-element.12.w_ref, ...), custom_call_target="tpu_custom_call" | custom-call | tf_op jit(solution)/shard_map/pallas_call | solution.py:494
